TPU v7x, 256 devices: a whole 4x4x8 slice. The times are simulated.
256 devices in a mesh: query: 16 (over y, x_lo, core), item: 16 (over z, x_hi).
Axes of the slice: x: 4 (x_hi: 2, x_lo: 2; x = x_hi * 2 + x_lo), y: 4, z: 8, core: 2. Of those that a mesh axis runs over, the one named last changes fastest.
Arguments:
- queries: bfloat16 [32768, 256], P('query'), may hold values from -45 to 45
- table: bfloat16 [1024, 128, 256], P('item'), may hold values from -6 to 6
- counts: int32 [1024, 128], P('item'), may hold values from 100 to 999
- lists: int32 [16, 16, 16], P('query', 'item'), may hold values from 0 to 63
- positives: int32 [32768], P('query'), may hold values from 0 to 131071
- positive_rows: bfloat16 [32768, 256], P(('query', 'item')), may hold values from -6 to 6
Outputs:
- losses: float32 [32768], P(('query', 'item'))
- query_grad: bfloat16 [32768, 256], P(('query', 'item'))
- positive_grad: bfloat16 [32768, 256], P(('query', 'item'))
- table_grad: bfloat16 [1024, 128, 256], P('item', 'query')
Inputs may be any that keep to these rules, and one draw needn't show every extreme that they name: lists[g, o, c] names a block of item shard o by its index within that shard.
All inputs are finite; a program needn't handle non-finite values.
Results may differ from a plain program's by a relative error of at most 0.0051.
Values may be sent and summed in bfloat16 or wider, within the bound.
A program may use at most 128 MiB of HBM per device.

v0:
```python
import jax
import jax.numpy as jnp
from jax import lax
from jax.sharding import PartitionSpec as P

score_scale = 0.125


def body(queries, table, counts, lists, positives, positive_rows):
    blk_dev, block, width = table.shape
    slice_rows = positive_rows.shape[0]
    item_index = lax.axis_index("item")
    shard_items = blk_dev * block
    item_logc = jnp.log(counts.astype(jnp.float32))
    owner = positives // shard_items
    local = jnp.clip(positives - item_index * shard_items, 0, shard_items - 1)
    found = jnp.where(owner == item_index, counts.reshape(-1)[local].astype(jnp.float32), 0.0)
    found_all = lax.psum(found, "item")
    pos_logc = jnp.log(found_all).astype(jnp.bfloat16)
    row_start = item_index * slice_rows
    mine_logc = lax.dynamic_slice_in_dim(pos_logc, row_start, slice_rows, 0)
    rows_all, logc_all = (
        lax.all_gather(positive_rows, "query", axis=0, tiled=True),
        lax.all_gather(mine_logc, "query", axis=0, tiled=True),
    )
    inbatch = (
        score_scale * jnp.einsum("qd,kd->qk", queries, rows_all, preferred_element_type=jnp.float32)
        - logc_all.astype(jnp.float32)[None, :]
    )
    chosen = lists.reshape(-1)
    keys = table[chosen].reshape(-1, width)
    key_logc = item_logc[chosen].reshape(-1)
    sampled = (
        score_scale * jnp.einsum("qd,kd->qk", queries, keys, preferred_element_type=jnp.float32)
        - key_logc[None, :]
    )
    local_top = jnp.maximum(jnp.max(sampled, axis=1), jnp.max(inbatch, axis=1))
    top = lax.pmax(local_top, "item")
    local_total = jnp.sum(jnp.exp(sampled - top[:, None]), axis=1) + jnp.sum(
        jnp.exp(inbatch - top[:, None]), axis=1
    )
    total = lax.psum(local_total, "item")
    lse = top + jnp.log(total)
    q_mine = lax.dynamic_slice_in_dim(queries, row_start, slice_rows, 0)
    label = score_scale * jnp.sum(
        q_mine.astype(jnp.float32) * positive_rows.astype(jnp.float32), axis=1
    ) - mine_logc.astype(jnp.float32)
    losses = lax.dynamic_slice_in_dim(lse, row_start, slice_rows, 0) - label
    p_sampled = jnp.exp(sampled - lse[:, None]).astype(jnp.bfloat16)
    p_inbatch = jnp.exp(inbatch - lse[:, None]).astype(jnp.bfloat16)
    query_term = score_scale * (
        jnp.dot(p_sampled, keys, preferred_element_type=jnp.float32)
        + jnp.dot(p_inbatch, rows_all, preferred_element_type=jnp.float32)
    )
    query_part = lax.psum_scatter(query_term, "item", scatter_dimension=0, tiled=True)
    query_grad = (query_part - score_scale * positive_rows.astype(jnp.float32)).astype(jnp.bfloat16)
    pos_part = lax.psum_scatter(
        score_scale
        * jnp.einsum("qk,qd->kd", p_inbatch, queries, preferred_element_type=jnp.float32),
        "query",
        scatter_dimension=0,
        tiled=True,
    )
    positive_grad = (pos_part - score_scale * q_mine.astype(jnp.float32)).astype(jnp.bfloat16)
    block_term = score_scale * jnp.einsum(
        "qk,qd->kd", p_sampled, queries, preferred_element_type=jnp.float32
    )
    block_term = block_term.reshape(-1, block, width)
    block_ids = jnp.arange(blk_dev, dtype=jnp.int32)[:, None]
    selector = (chosen[None, :] == block_ids).astype(jnp.float32)
    dense_term = jnp.einsum("bc,crd->brd", selector, block_term, precision=lax.Precision.HIGHEST)
    table_part = lax.psum_scatter(dense_term, "query", scatter_dimension=1, tiled=True)
    return (losses, query_grad, positive_grad, table_part.astype(jnp.bfloat16))


def solution(mesh):
    return jax.shard_map(
        body,
        mesh=mesh,
        in_specs=(
            P("query", None),
            P("item", None, None),
            P("item", None),
            P("query", "item", None),
            P("query"),
            P(("query", "item"), None),
        ),
        out_specs=(
            P(("query", "item")),
            P(("query", "item"), None),
            P(("query", "item"), None),
            P("item", "query", None),
        ),
        check_vma=False,
    )
```

profile of v0, /device:TPU:32, one launch (start us, length us, event | category | flops | bytes accessed | tf_op | source)
XLA Modules:
  0.0 586.1 jit_solution(12399727023551655054)
XLA Ops:
  7.2 0.0 copy-start.1
  7.2 0.0 all-gather.3.cloned.1.call-start
  7.2 0.7 all-gather.3.cloned.1.call-update
  7.9 0.0 reduce-scatter.6.cloned.1.call-start
  8.0 0.7 fusion.12
  8.7 10.3 %gather_fusion.2 = s32[2048]{0:T(1024)S(1)} fusion(s32[8192]{0:T(1024)} %bitcast.25, s32[2048]{0:T(1024)S(1)} %fusion.12), kind=kCustom, calls=%fused_computation.2 | custom fusion | bytes 24576 | tf_op jit(solution)/shard_map/gather | solution.py:17
  19.0 0.7 convert_select_fusion
  19.7 42.9 %psum.14 = f32[2048]{0:T(1024)S(1)} all-reduce(f32[2048]{0:T(1024)S(1)} %convert_select_fusion), channel_id=1, replica_groups=mesh['query'=16,'item'=16] {'item'}, use_global_device_ids=true, to_apply=%region_1.2 | all-reduce | flops 2048 | bytes 16384 | tf_op jit(solution)/shard_map/psum | solution.py:18
  62.6 0.1 fusion.19
  62.7 18.9 %all-gather = bf16[16,1,128]{2,1,0:T(2,128)(2,1)S(1)} all-gather(bf16[1,1,128]{2,1,0:T(2,128)(2,1)S(1)} %fusion.19), channel_id=1, replica_groups=mesh['query'=16,'item'=16] {'query'}, dimensions={0}, use_global_device_ids=true | all-gather | bytes 4352 | tf_op jit(solution)/shard_map/all_gather | solution.py:24
  81.6 0.7 fusion.17
  82.2 0.8 convert_log_fusion
  83.0 0.6 gather_fusion.1
  83.6 2.8 gather_fusion
  86.4 8.3 %fusion = (f32[2048]{0:T(1024)S(1)}, f32[2048,2048]{1,0:T(8,128)}) fusion(f32[2048]{0:T(1024)S(1)} %bitcast.31, bf16[2048,256]{1,0:T(8,128)(2,1)S(1)} %bitcast.28, bf16[2048,256]{1,0:T(8,128)(2,1)} %param.6), kind=kOutput, calls=%fused_computation.9 | convolution fusion | flops 2160064512 | bytes 18890752 | tf_op jit(solution)/shard_map/qd,kd->qk/dot_general | solution.py:34
  94.6 0.0 all-gather.3.cloned.1.call-done
  94.6 0.0 copy-done.1
  94.6 8.3 %fusion.1 = (f32[2048]{0:T(1024)S(1)}, f32[2048,2048]{1,0:T(8,128)}) fusion(f32[2048]{0:T(1024)S(1)} %bitcast.34, bf16[2048,256]{1,0:T(8,128)(2,1)S(1)} %copy-done.1, bf16[2048,256]{1,0:T(8,128)(2,1)} %all-gather.3.cloned.1.call-done), kind=kOutput, calls=%fused_computation.10 | convolution fusion | flops 2160064512 | bytes 18890752 | tf_op jit(solution)/shard_map/qd,kd->qk/dot_general | solution.py:27
  102.9 37.5 %pmax.7 = f32[2048]{0:T(1024)S(1)} all-reduce(f32[2048]{0:T(1024)S(1)} %max.9), channel_id=1, replica_groups=mesh['query'=16,'item'=16] {'item'}, use_global_device_ids=true, to_apply=%region_3.4 | all-reduce | flops 2048 | bytes 16384 | tf_op jit(solution)/shard_map/pmax | solution.py:38
  140.4 13.1 %exponential_reduce_fusion = (f32[2048]{0:T(1024)S(1)}, f32[2048]{0:T(1024)S(1)}) fusion(f32[2048,2048]{1,0:T(8,128)} %get-tuple-element.24, f32[2048]{0:T(1024)S(1)} %pmax.7, f32[2048]{0:T(1024)S(1)} %bitcast.35, f32[2048]{0:T(1024)S(1)} %bitcast.32, f32[2048,2048]{1,0:T(8,128)} %get-tuple-element.22), kind=kLoop, calls=%fused_computation.5 | loop fusion | flops 33550336 | bytes 33595392 | tf_op jit(solution)/shard_map/reduce_sum | solution.py:39
  153.5 40.3 %psum.15 = f32[2048]{0:T(1024)S(1)} all-reduce(f32[2048]{0:T(1024)S(1)} %add.43), channel_id=1, replica_groups=mesh['query'=16,'item'=16] {'item'}, use_global_device_ids=true, to_apply=%region_6.7 | all-reduce | flops 2048 | bytes 16384 | tf_op jit(solution)/shard_map/psum | solution.py:42
  193.9 9.3 %convolution_multiply_fusion.1 = f32[2048,256]{1,0:T(8,128)} fusion(bf16[2048,256]{1,0:T(8,128)(2,1)S(1)} %copy-done.1, f32[2048,2048]{1,0:T(8,128)} %get-tuple-element.24, f32[2048]{0:T(1024)S(1)} %log_add_fusion, f32[2048]{0:T(1024)S(1)} %bitcast.36), kind=kOutput, calls=%fused_computation.12 | convolution fusion | flops 2164785152 | bytes 19939328 | tf_op jit(solution)/shard_map/qk,qd->kd/dot_general | solution.py:59
  203.1 0.0 reduce-scatter.6.cloned.1.call-update
  203.2 0.0 copy-start.2
  203.2 0.2 reduce-scatter.4.cloned.1.call-start
  203.4 0.0 slice-start
  203.4 0.0 slice-start.1
  203.4 0.0 slice-start.2
  203.4 8.5 %exponential_convert_fusion.1 = bf16[2048,2048]{1,0:T(8,128)(2,1)S(1)} fusion(f32[2048,2048]{1,0:T(8,128)} %get-tuple-element.22, f32[2048]{0:T(1024)S(1)} %log_add_fusion, f32[2048]{0:T(1024)S(1)} %bitcast.33), kind=kLoop, calls=%fused_computation.4 | loop fusion | flops 16777216 | bytes 25182208 | tf_op jit(solution)/shard_map/convert
  211.9 0.0 copy-start
  211.9 3.2 copy-done
  215.1 0.0 slice-start.3
  215.1 2.6 fusion.20
  217.8 0.0 copy-done.2
  217.8 0.0 slice-done
  217.8 0.0 slice-done.1
  217.8 0.0 slice-done.2
  217.8 0.0 slice-done.3
  217.8 4.9 fusion.2
  222.7 0.0 copy-start.4
  222.7 0.0 reduce-scatter.4.cloned.1.call-update
  222.8 0.0 copy-start.3
  222.8 0.0 reduce-scatter.8.cloned.1.call-start
  222.8 5.9 %convolution_multiply_fusion = f32[2048,256]{1,0:T(8,128)S(1)} fusion(bf16[2048,2048]{1,0:T(8,128)(2,1)} %copy-done, bf16[2048,256]{1,0:T(8,128)(2,1)S(1)} %copy-done.1), kind=kOutput, calls=%fused_computation.11 | convolution fusion | flops 2148007936 | bytes 11534336 | tf_op jit(solution)/shard_map/qk,qd->kd/dot_general | solution.py:65
  228.7 0.0 copy-done.4
  228.7 6.0 %fusion.3 = f32[64,128,256]{2,0,1:T(8,128)} fusion(f32[16,128,256]{2,1,0:T(8,128)S(1)} %bitcast.30, s32[16]{0:T(128)S(1)} %bitcast.38), kind=kOutput, calls=%fused_computation.15 | convolution fusion | flops 402654208 | bytes 10485824 | tf_op jit(solution)/shard_map/bc,crd->brd/dot_general | solution.py:71
  234.7 0.0 reduce-scatter.8.cloned.1.call-update
  234.7 32.0 %reduce-scatter.6.cloned.1.call-done = f32[128,256]{1,0:T(8,128)} async-done(((f32[2048,256]{1,0:T(8,128)}), f32[128,256]{1,0:T(8,128)}) %reduce-scatter.6.cloned.1.call-update) | async-done | bytes 131088 | tf_op jit(solution)/shard_map/reduce_scatter | solution.py:57
  266.8 209.1 %reduce-scatter.4.cloned.1.call-done = f32[128,256]{1,0:T(8,128)} async-done(((f32[2048,256]{1,0:T(8,128)}), f32[128,256]{1,0:T(8,128)}) %reduce-scatter.4.cloned.1.call-update) | async-done | bytes 131088 | tf_op jit(solution)/shard_map/reduce_scatter | solution.py:55
  475.8 0.0 copy-done.3
  475.8 1.7 fusion.6
  477.5 0.6 subtract_subtract_fusion
  478.1 99.5 %reduce-scatter.8.cloned.1.call-done = f32[64,8,256]{2,0,1:T(8,128)} async-done(((f32[64,128,256]{2,0,1:T(8,128)}), f32[64,8,256]{2,0,1:T(8,128)}) %reduce-scatter.8.cloned.1.call-update) | async-done | bytes 524304 | tf_op jit(solution)/shard_map/reduce_scatter | solution.py:72
  577.6 1.1 convert_element_type.47
  578.7 0.9 copy.18
  (6 shorter events, 0.0 us)
Async XLA Ops:
  7.2 87.5 %copy-start.1 = (bf16[2048,256]{1,0:T(8,128)(2,1)S(1)}, bf16[2048,256]{1,0:T(8,128)(2,1)}, u32[]{:S(2)}) copy-start(bf16[2048,256]{1,0:T(8,128)(2,1)} %param.6) | copy-start | bytes 3145732
  7.2 87.5 %all-gather.3.cloned.1.call-start = ((), (), s32[]{:S(2)}) async-start(), calls=%async_computation.3 | async-start | bytes 1114112 | tf_op jit(solution)/shard_map/all_gather | solution.py:23
  7.9 258.8 %reduce-scatter.6.cloned.1.call-start = ((), (), s32[]{:S(2)}) async-start(), calls=%async_computation.5 | async-start | bytes 2228224 | tf_op jit(solution)/shard_map/reduce_scatter | solution.py:57
  203.2 14.6 %copy-start.2 = (bf16[2048,256]{1,0:T(8,128)(2,1)S(1)}, bf16[2048,256]{1,0:T(8,128)(2,1)}, u32[]{:S(2)}) copy-start(bf16[2048,256]{1,0:T(8,128)(2,1)} %all-gather.3.cloned.1.call-done) | copy-start | bytes 3145732
  203.2 272.7 %reduce-scatter.4.cloned.1.call-start = ((), (), s32[]{:S(2)}) async-start(), calls=%async_computation.4 | async-start | bytes 2228224 | tf_op jit(solution)/shard_map/reduce_scatter | solution.py:55
  203.4 14.4 %slice-start = ((s8[16777216]{0:T(1024)(128)(4,1)}), s8[4194304]{0:T(1024)(128)(4,1)S(1)}, s32[]{:S(2)}) async-start(s8[16777216]{0:T(1024)(128)(4,1)} %bitcast.26), calls=%async_computation.7 | async-start | bytes 8388608
  203.4 14.4 %slice-start.1 = ((s8[16777216]{0:T(1024)(128)(4,1)}), s8[4194304]{0:T(1024)(128)(4,1)S(1)}, s32[]{:S(2)}) async-start(s8[16777216]{0:T(1024)(128)(4,1)} %bitcast.26), calls=%async_computation.8 | async-start | bytes 8388608
  203.4 14.4 %slice-start.2 = ((s8[16777216]{0:T(1024)(128)(4,1)}), s8[4194304]{0:T(1024)(128)(4,1)S(1)}, s32[]{:S(2)}) async-start(s8[16777216]{0:T(1024)(128)(4,1)} %bitcast.26), calls=%async_computation.9 | async-start | bytes 8388608
  211.9 3.2 copy-start
  215.1 2.7 slice-start.3
  222.7 6.0 %copy-start.4 = (s32[1,1,16]{2,1,0:T(1,128)S(1)}, s32[1,1,16]{2,1,0:T(1,128)}, u32[]{:S(2)}) copy-start(s32[1,1,16]{2,1,0:T(1,128)} %param.9) | copy-start | bytes 196
  222.8 253.1 %copy-start.3 = (bf16[128,256]{1,0:T(8,128)(2,1)S(1)}, bf16[128,256]{1,0:T(8,128)(2,1)}, u32[]{:S(2)}) copy-start(bf16[128,256]{1,0:T(8,128)(2,1)} %param.11) | copy-start | bytes 196612
  222.8 354.9 %reduce-scatter.8.cloned.1.call-start = ((), (), s32[]{:S(2)}) async-start(), calls=%async_computation.6 | async-start | bytes 8912896 | tf_op jit(solution)/shard_map/reduce_scatter | solution.py:72
Sparse Core Ops, SparseCore 0:
  9.9 37.5 all-gather.2
  203.3 63.4 reduce-scatter.5
  270.6 205.1 reduce-scatter.3
  478.2 99.3 reduce-scatter.7
where the time goes:
time: 587 us; the launch traced here: 586 us
  waiting for transfers between devices  341 us (58%)
  blocking collectives  140 us (24%)
  matrix products  45.2 us (8%)
  other arithmetic  27.9 us (5%)
  local copies, waits for them, and re-layouts  17.8 us (3%)
  between operations  14 us (2%)
    reduce_scatter x1, waiting for transfers between devices, body(): lax.psum_scatter(query_term, 'item', scatter_dimension=0, tiled=True)  209 us
    reduce_scatter x1, waiting for transfers between devices, body(): lax.psum_scatter(dense_term, 'query', scatter_dimension=1, tiled=True)  99.5 us
    psum x1, blocking collectives, body(): found_all = lax.psum(found, 'item')  42.9 us
    psum x1, blocking collectives, body(): total = lax.psum(local_total, 'item')  40.3 us
    pmax x1, blocking collectives, body(): top = lax.pmax(local_top, 'item')  37.5 us
    reduce_scatter x1, waiting for transfers between devices, body(): lax.psum_scatter(score_scale * jnp.einsum('qk,qd->kd', p_inbatch, queries...  32 us
    all_gather x1, blocking collectives, body(): lax.all_gather(mine_logc, 'query', axis=0, tiled=True)  18.9 us
    reduce_sum x1, other arithmetic, body(): jnp.sum(jnp.exp(inbatch - top[:, None]), axis=1)  13.1 us
  transfers between devices with their start and end apart: 4, of which 3 were waited for; matrix products, arithmetic and copies ran while one was open for 9% of the time, Pallas kernels for 0%

commit v1 on v0

v1 whole, which is shorter than its diff:
```python
import functools

import jax
import jax.numpy as jnp
from jax import lax
from jax.experimental import pallas as pl
from jax.experimental.pallas import tpu as pltpu
from jax.sharding import PartitionSpec as P

MESH = pl.DeviceIdType.MESH
F32, BF16, I32 = jnp.float32, jnp.bfloat16, jnp.int32
LOG2E = 1.4426950408889634
LN2 = 0.6931471805599453
SCALE = 0.125
TQ = 256
KC = 256
KG = 512


def iota(shape, dim):
    return lax.broadcasted_iota(I32, shape, dim)


def kernel(
    nq,
    ni,
    table_hbm,
    q_ref,
    counts_ref,
    lists_ref,
    pos_ref,
    rows_ref,
    loss_ref,
    qg_ref,
    pg_ref,
    tg_ref,
    table_v,
    keys_s,
    keys_i,
    lc_s,
    lc_i,
    e_s,
    e_i,
    s_a,
    s_b,
    m_a,
    m_b,
    mx_s,
    mx_i,
    sm_s,
    sm_i,
    g_s,
    g_i,
    wq_s,
    wq_i,
    tp,
    cnt_send,
    cnt_recv,
    log_send,
    log_recv,
    key_send,
    key_recv,
    stat_send,
    stat_recv,
    lse_send,
    lse_recv,
    b_send,
    b_recv,
    c_send,
    c_recv,
    d_send,
    d_recv,
    hot,
    table_sem,
    ssem,
    rsem,
):
    qi, ii = lax.axis_index("query"), lax.axis_index("item")
    nblk, block, width = table_v.shape
    cap = lists_ref.shape[2]
    nqry = q_ref.shape[0]
    sl = rows_ref.shape[0]
    per = block // nq
    dest = cap * per
    nk = keys_s.shape[0]
    ntile = nqry // TQ

    def to(axis, me, n, src, dst, x):
        def copy(peer, slot):
            return pltpu.make_async_remote_copy(
                src_ref=src(peer),
                dst_ref=dst.at[slot],
                send_sem=ssem.at[x, peer],
                recv_sem=rsem.at[x, slot],
                device_id={axis: peer},
                device_id_type=MESH,
            )

        def each(act):
            def step(off, _):
                act(lax.rem(me + off, n))
                return 0

            lax.fori_loop(1, n, step, 0)

        class X:
            start_to = staticmethod(lambda p: copy(p, me).start())
            start = staticmethod(lambda: each(X.start_to))
            wait_recv = staticmethod(lambda: each(lambda p: copy(p, p).wait_recv()))
            wait_send = staticmethod(lambda: each(lambda p: copy(p, me).wait_send()))

        return X

    def rows_of(ref, n):
        return lambda p: ref.at[pl.ds(pl.multiple_of(p * n, n), n)]

    x_row = to("query", qi, nq, lambda p: rows_ref, keys_i, 0)
    x_cnt = to("item", ii, ni, lambda p: cnt_send.at[p], cnt_recv, 1)
    x_log = to("query", qi, nq, lambda p: log_send, log_recv, 2)
    x_key = to("query", qi, nq, lambda p: key_send, key_recv, 3)
    x_stat = to("item", ii, ni, lambda p: stat_send.at[p], stat_recv, 4)
    x_lse = to("item", ii, ni, lambda p: lse_send, lse_recv, 5)
    x_b = to("item", ii, ni, lambda p: b_send.at[p], b_recv, 6)
    x_c = to("query", qi, nq, lambda p: c_send.at[p], c_recv, 7)
    x_d = to("query", qi, nq, lambda p: d_send.at[p], d_recv, 8)

    table_in = pltpu.make_async_copy(table_hbm, table_v, table_sem)
    table_in.start()
    barrier = pltpu.get_barrier_semaphore()

    def greet(axis, me, n):
        def step(off, _):
            pl.semaphore_signal(
                barrier, inc=1, device_id={axis: lax.rem(me + off, n)}, device_id_type=MESH
            )
            return 0

        lax.fori_loop(1, n, step, 0)

    greet("query", qi, nq)
    greet("item", ii, ni)

    lane = iota((8, dest), 1)
    lane_c, lane_r = lane // per, lane % per
    lane_key = lane_r
    for c in range(cap):
        lane_key = lane_key + jnp.where(lane_c == c, lists_ref[0, 0, c] * per, 0)
    key_send[...] = lane_key
    key_recv[qi] = lane_key

    cnt = counts_ref[...]
    halves = jnp.concatenate([cnt >> 8, cnt & 255], axis=0).astype(F32)
    by_row = jnp.transpose(halves).astype(BF16)

    def count_slice(s, _):
        p = pos_ref[pl.ds(s, 1), :]
        blk = (p >> 7) - ii * nblk
        one = (iota((nblk, sl), 0) == blk).astype(F32)
        both = jnp.concatenate([one * 256.0, one], axis=0).astype(BF16)
        found = jnp.dot(by_row, both, preferred_element_type=F32)
        found = jnp.where(iota((block, sl), 0) == (p & (block - 1)), found, 0.0)
        cnt_send[s] = jnp.broadcast_to(jnp.sum(found, axis=0, keepdims=True), (8, sl))
        return 0

    lax.fori_loop(0, ni, count_slice, 0)
    cnt_recv[ii] = cnt_send[ii]
    keys_i[qi] = rows_ref[...]

    pl.semaphore_wait(barrier, nq + ni - 2)
    x_row.start()
    x_cnt.start()
    x_key.start()

    tp[...] = jnp.zeros_like(tp)
    for c in range(cap):
        row = counts_ref[pl.ds(lists_ref[0, 0, c], 1), :].astype(F32)
        tp[c : c + 1, :] = jnp.log(row) * LOG2E
    cols = jnp.transpose(tp[...])
    for c in range(cap):
        col = jnp.broadcast_to(cols[:, c : c + 1], (block, 128))
        lc_s[:, c * per : (c + 1) * per, :] = col.reshape(nq, per, 128)
    table_in.wait()
    pair = max(1, 16 // per)
    for c in range(0, cap, pair):
        parts = [
            table_v[lists_ref[0, 0, c + j]].astype(F32).reshape(nq, per, width)
            for j in range(pair)
        ]
        both = jnp.concatenate(parts, axis=1) if pair > 1 else parts[0]
        keys_s[:, c * per : (c + pair) * per, :] = both.astype(BF16)

    def chunks(ref, size):
        n, rows = ref.shape[0], ref.shape[1]
        step = max(1, min(n, size // rows))
        return [(j, j + step) for j in range(0, n, step)], rows

    def scores(keys, lc, e, mx, sm):
        spans, rows = chunks(keys, KC)

        def tile_of(t):
            return q_ref[pl.ds(pl.multiple_of(t * TQ, TQ), TQ), :]

        def both(t_new, s_new, m_new, t_old, s_old, m_old):
            if t_new is not None:
                q = tile_of(t_new)
                m8 = jnp.full((8, TQ), -jnp.inf, F32)
            if t_old is not None:
                top = jnp.max(m_old[...], axis=0, keepdims=True)
                at = pl.ds(pl.multiple_of(t_old * TQ, TQ), TQ)
                s8 = jnp.zeros((8, TQ), F32)
            for lo, hi in spans:
                n = (hi - lo) * rows
                if t_new is not None:
                    k = keys[lo:hi].reshape(n, width)
                    d = lax.dot_general(
                        k, q, (((1,), (1,)), ((), ())), preferred_element_type=F32
                    )
                    c = lc[lo:hi].reshape(n, 128)
                    s = d * (SCALE * LOG2E) - jnp.concatenate([c] * (TQ // 128), axis=1)
                    s_new[lo * rows : hi * rows, :] = s
                    m8 = jnp.maximum(m8, jnp.max(s.reshape(n // 8, 8, TQ), axis=0))
                if t_old is not None:
                    x = jnp.exp2(s_old[lo * rows : hi * rows, :] - top)
                    s8 = s8 + jnp.sum(x.reshape(n // 8, 8, TQ), axis=0)
                    e[lo * rows : hi * rows, at] = x.astype(BF16)
            if t_new is not None:
                m_new[...] = m8
            if t_old is not None:
                mx[:, at] = top
                sm[:, at] = jnp.sum(s8, axis=0, keepdims=True)

        both(0, s_a, m_a, None, None, None)

        def pair_of_tiles(u, _):
            both(2 * u + 1, s_b, m_b, 2 * u, s_a, m_a)
            both(2 * u + 2, s_a, m_a, 2 * u + 1, s_b, m_b)
            return 0

        lax.fori_loop(0, ntile // 2 - 1, pair_of_tiles, 0)
        both(ntile - 1, s_b, m_b, ntile - 2, s_a, m_a)
        both(None, None, None, ntile - 1, s_b, m_b)

    def query_grads(keys, e, g):
        n = keys.shape[0] * keys.shape[1]

        def step(t, _):
            at = pl.ds(pl.multiple_of(t * TQ, TQ), TQ)
            g[at, :] = lax.dot_general(
                e[:, at],
                keys[...].reshape(n, width),
                (((0,), (0,)), ((), ())),
                preferred_element_type=F32,
            )
            return 0

        lax.fori_loop(0, ntile, step, 0)

    scores(keys_s, lc_s, e_s, mx_s, sm_s)

    x_cnt.wait_recv()
    total = cnt_recv[0]
    for o in range(1, ni):
        total = total + cnt_recv[o]
    mine_logc = jnp.log(total).astype(BF16).astype(F32)
    log_send[...] = mine_logc
    log_recv[qi] = mine_logc
    x_log.start()
    query_grads(keys_s, e_s, g_s)

    x_log.wait_recv()
    for g in range(nq):
        tp[g : g + 1, :] = log_recv[g, 0:1, :] * LOG2E
    cols = jnp.transpose(tp[...])
    for g in range(nq):
        lc_i[g] = jnp.broadcast_to(cols[:, g : g + 1], (sl, 128))
    x_row.wait_recv()
    scores(keys_i, lc_i, e_i, mx_i, sm_i)

    row8 = iota((8, sl), 0)
    for o in range(ni):
        at = slice(o * sl, (o + 1) * sl)
        top = jnp.maximum(mx_s[:, at], mx_i[:, at])
        part = sm_s[:, at] * jnp.exp2(mx_s[:, at] - top) + sm_i[:, at] * jnp.exp2(
            mx_i[:, at] - top
        )
        stat_send[o] = jnp.where(row8 == 0, top, part)
    stat_recv[ii] = stat_send[ii]
    x_stat.start()
    query_grads(keys_i, e_i, g_i)
    x_stat.wait_recv()
    top = stat_recv[0, 0:1, :]
    for o in range(1, ni):
        top = jnp.maximum(top, stat_recv[o, 0:1, :])
    part = jnp.zeros((1, sl), F32)
    for o in range(ni):
        part = part + stat_recv[o, 1:2, :] * jnp.exp2(stat_recv[o, 0:1, :] - top)
    lse2 = top + jnp.log(part) * LOG2E
    lse_send[...] = jnp.broadcast_to(lse2, (8, sl))
    lse_recv[ii] = lse_send[...]
    x_lse.start()

    mine = pl.ds(pl.multiple_of(ii * sl, sl), sl)
    q_mine = q_ref[mine, :].astype(F32)
    r_mine = rows_ref[...].astype(F32)
    label = SCALE * jnp.sum(q_mine * r_mine, axis=1, keepdims=True)
    label = jnp.sum(
        jnp.where(iota((sl, sl), 0) == iota((sl, sl), 1), label, 0.0), axis=0, keepdims=True
    )
    loss_ref[...] = lse2 * LN2 - (label - mine_logc[0:1, :])

    x_key.wait_recv()
    for g in range(nq):
        want = iota((nblk * per, dest), 0)
        hot[:, g * dest : (g + 1) * dest] = jnp.where(
            want == key_recv[g, 0:1, :], 1.0, 0.0
        ).astype(BF16)

    x_lse.wait_recv()
    for o in range(ni):
        at = slice(o * sl, (o + 1) * sl)
        lse = lse_recv[o, 0:1, :]
        tp[o : o + 1, :] = jnp.exp2(mx_s[:, at] - lse) * SCALE
        tp[ni + o : ni + o + 1, :] = jnp.exp2(mx_i[:, at] - lse) * SCALE
    cols = jnp.transpose(tp[...])
    for o in range(ni):
        at = slice(o * sl, (o + 1) * sl)
        w_s, w_i = cols[:, o : o + 1], cols[:, ni + o : ni + o + 1]
        q = q_ref[at, :].astype(F32)
        wq_s[at, :] = (q * w_s).astype(BF16)
        wq_i[at, :] = (q * w_i).astype(BF16)
        b_send[o] = (g_s[at, :] * w_s + g_i[at, :] * w_i).astype(BF16)
    x_b.start()

    def key_grads(e, wq, out, start, me):
        n, rows = out.shape[0], out.shape[1]
        step = max(1, min(n, KG // rows))

        def one(j, _):
            at = pl.ds(pl.multiple_of(j * step * rows, step * rows), step * rows)
            k = jnp.dot(e[at, :], wq[...], preferred_element_type=F32)
            k = k.astype(BF16).reshape(step, rows, width)
            for h in range(step):
                p = j * step + h
                out[p] = k[h]

                @pl.when(p != me)
                def _():
                    start(p)

            return 0

        lax.fori_loop(0, n // step, one, 0)

    key_grads(e_s, wq_s, d_send, x_d.start_to, qi)
    d_recv[qi] = d_send[qi]
    key_grads(e_i, wq_i, c_send, x_c.start_to, qi)
    c_recv[qi] = c_send[qi]
    b_recv[ii] = b_send[ii]

    def added(ref, n):
        def step(o, acc):
            return acc + ref[o].astype(F32)

        return lax.fori_loop(0, n, step, jnp.zeros((sl, width), F32))

    x_b.wait_recv()
    qg_ref[...] = (added(b_recv, ni) - SCALE * r_mine).astype(BF16)
    x_d.wait_recv()
    grads = jnp.dot(
        hot[...], d_recv[...].reshape(nq * dest, width), preferred_element_type=F32
    )
    tg_ref[...] = grads.reshape(nblk, per, width).astype(BF16)
    x_c.wait_recv()
    pg_ref[...] = (added(c_recv, nq) - SCALE * q_mine).astype(BF16)

    for x in (x_row, x_cnt, x_log, x_key, x_stat, x_lse, x_b, x_c, x_d):
        x.wait_send()


def solution(mesh):
    nq, ni = mesh.shape["query"], mesh.shape["item"]

    def step(queries, table, counts, lists, positives, positive_rows):
        nblk, block, width = table.shape
        nqry, sl, cap = queries.shape[0], positive_rows.shape[0], lists.shape[2]
        per = block // nq
        dest = cap * per
        nk_s, nk_i = nq * dest, nq * sl
        most = max(nk_s, nk_i)
        vm, dma = pltpu.VMEM, pltpu.SemaphoreType.DMA
        whole = pl.BlockSpec(memory_space=vm)
        loss, qg, pg, tg = pl.pallas_call(
            functools.partial(kernel, nq, ni),
            out_shape=(
                jax.ShapeDtypeStruct((1, sl), F32),
                jax.ShapeDtypeStruct((sl, width), BF16),
                jax.ShapeDtypeStruct((sl, width), BF16),
                jax.ShapeDtypeStruct((nblk, per, width), BF16),
            ),
            in_specs=[
                pl.BlockSpec(memory_space=pl.ANY),
                whole,
                whole,
                pl.BlockSpec(memory_space=pltpu.SMEM),
                whole,
                whole,
            ],
            out_specs=[whole] * 4,
            scratch_shapes=[
                vm((nblk, block, width), BF16),
                vm((nq, dest, width), BF16),
                vm((nq, sl, width), BF16),
                vm((nq, dest, 128), F32),
                vm((nq, sl, 128), F32),
                vm((nk_s, nqry), BF16),
                vm((nk_i, nqry), BF16),
                vm((most, TQ), F32),
                vm((most, TQ), F32),
                vm((8, TQ), F32),
                vm((8, TQ), F32),
                vm((1, nqry), F32),
                vm((1, nqry), F32),
                vm((1, nqry), F32),
                vm((1, nqry), F32),
                vm((nqry, width), F32),
                vm((nqry, width), F32),
                vm((nqry, width), BF16),
                vm((nqry, width), BF16),
                vm((128, 128), F32),
                vm((ni, 8, sl), F32),
                vm((ni, 8, sl), F32),
                vm((8, sl), F32),
                vm((nq, 8, sl), F32),
                vm((8, dest), I32),
                vm((nq, 8, dest), I32),
                vm((ni, 8, sl), F32),
                vm((ni, 8, sl), F32),
                vm((8, sl), F32),
                vm((ni, 8, sl), F32),
                vm((ni, sl, width), BF16),
                vm((ni, sl, width), BF16),
                vm((nq, sl, width), BF16),
                vm((nq, sl, width), BF16),
                vm((nq, dest, width), BF16),
                vm((nq, dest, width), BF16),
                vm((nblk * per, nq * dest), BF16),
                dma,
                dma((9, max(nq, ni))),
                dma((9, max(nq, ni))),
            ],
            compiler_params=pltpu.CompilerParams(
                collective_id=0, has_side_effects=True, vmem_limit_bytes=60 << 20
            ),
        )(table, queries, counts, lists, positives.reshape(-1, 128), positive_rows)
        return loss.reshape(sl), qg, pg, tg

    return jax.shard_map(
        step,
        mesh=mesh,
        in_specs=(
            P("query", None),
            P("item", None, None),
            P("item", None),
            P("query", "item", None),
            P("query"),
            P(("query", "item"), None),
        ),
        out_specs=(
            P(("query", "item")),
            P(("query", "item"), None),
            P(("query", "item"), None),
            P("item", "query", None),
        ),
        check_vma=False,
    )
```

time: 587 us -> 96.9 us (0.17)
  the two profiles are of different devices: /device:TPU:32 before, /device:TPU:29 now
where the time goes in v1:
time: 96.9 us; the launch traced here: 96.7 us
  Pallas kernels  90.3 us (93%)
  local copies, waits for them, and re-layouts  5.73 us (6%)
    pallas_call x1, Pallas kernels, step(): pl.pallas_call(functools.partial(kernel, nq, ni), out_shape=(jax.ShapeDty...  90.3 us
    unnamed x4, local copies, waits for them, and re-layouts  5.73 us

profile of v1, /device:TPU:29, one launch (start us, length us, event | category | flops | bytes accessed | tf_op | source)
XLA Modules:
  0.0 96.7 jit_solution(14721783499151413300)
XLA Ops:
  0.6 90.3 %shard_map.93 = (f32[1,128]{1,0:T(1,128)}, bf16[128,256]{1,0:T(8,128)(2,1)}, bf16[128,256]{1,0:T(8,128)(2,1)}, bf16[64,8,256]{2,1,0:T(8,128)(2,1)}) custom-call(bf16[64,128,256]{2,1,0:T(8,128)(2,1)} %table_hbm.1, bf16[2048,256]{1,0:T(8,128)(2,1)} %q_ref.1, s32[64,128]{1,0:T(8,128)} %counts_ref.1, s32[1,1,16]{2,1,0:T(1,128)} %lists_ref.1, s32[16,128]{1,0:T(8,128)} %bitcast.2, ...), custom_call_target="tpu_custom_call" | custom-call | tf_op jit(solution)/shard_map/pallas_call | solution.py:392
  91.0 1.1 %copy.14 = f32[128]{0:T(128)} copy(f32[128]{0:T(128)} %bitcast.3) | data formatting | bytes 1024
  92.1 1.5 %copy.15 = bf16[128,256]{1,0:T(8,128)(2,1)} copy(bf16[128,256]{1,0:T(8,128)(2,1)} %get-tuple-element.17) | data formatting | bytes 131072
  93.6 1.5 %copy.16 = bf16[128,256]{1,0:T(8,128)(2,1)} copy(bf16[128,256]{1,0:T(8,128)(2,1)} %get-tuple-element.18) | data formatting | bytes 131072
  95.0 1.7 %copy.17 = bf16[64,8,256]{2,1,0:T(8,128)(2,1)} copy(bf16[64,8,256]{2,1,0:T(8,128)(2,1)} %get-tuple-element.19) | data formatting | bytes 524288

commit v2 on v1

--- a/solution.py
+++ b/solution.py
@@ -25,16 +25,21 @@
     nq,
     ni,
     table_hbm,
+    q_hbm,
+    counts_hbm,
+    lists_hbm,
+    pos_hbm,
+    rows_hbm,
+    loss_ref,
+    qg_ref,
+    pg_ref,
+    tg_ref,
+    table_v,
     q_ref,
     counts_ref,
     lists_ref,
     pos_ref,
     rows_ref,
-    loss_ref,
-    qg_ref,
-    pg_ref,
-    tg_ref,
-    table_v,
     keys_s,
     keys_i,
     lc_s,
@@ -64,16 +69,22 @@
     stat_recv,
     lse_send,
     lse_recv,
-    b_send,
-    b_recv,
+    ring_send,
+    ring_recv,
+    half_send,
+    half_recv,
+    core_send,
+    core_recv,
     c_send,
     c_recv,
     d_send,
     d_recv,
     hot,
-    table_sem,
+    in_sem,
     ssem,
     rsem,
+    ring_ssem,
+    ring_rsem,
 ):
     qi, ii = lax.axis_index("query"), lax.axis_index("item")
     nblk, block, width = table_v.shape
@@ -84,6 +95,12 @@
     dest = cap * per
     nk = keys_s.shape[0]
     ntile = nqry // TQ
+    nchip, nz = nq // 2, ni // 2
+    chip, core = qi // 2, lax.rem(qi, 2)
+    twin = qi + 1 - 2 * core
+    z, xh = ii // 2, lax.rem(ii, 2)
+    mirror = ii + 1 - 2 * xh
+    reach = nz // 2
 
     def to(axis, me, n, src, dst, x):
         def copy(peer, slot):
@@ -111,21 +128,46 @@
 
         return X
 
-    def rows_of(ref, n):
-        return lambda p: ref.at[pl.ds(pl.multiple_of(p * n, n), n)]
-
-    x_row = to("query", qi, nq, lambda p: rows_ref, keys_i, 0)
     x_cnt = to("item", ii, ni, lambda p: cnt_send.at[p], cnt_recv, 1)
     x_log = to("query", qi, nq, lambda p: log_send, log_recv, 2)
     x_key = to("query", qi, nq, lambda p: key_send, key_recv, 3)
     x_stat = to("item", ii, ni, lambda p: stat_send.at[p], stat_recv, 4)
     x_lse = to("item", ii, ni, lambda p: lse_send, lse_recv, 5)
-    x_b = to("item", ii, ni, lambda p: b_send.at[p], b_recv, 6)
-    x_c = to("query", qi, nq, lambda p: c_send.at[p], c_recv, 7)
-    x_d = to("query", qi, nq, lambda p: d_send.at[p], d_recv, 8)
-
-    table_in = pltpu.make_async_copy(table_hbm, table_v, table_sem)
-    table_in.start()
+    x_d = to("query", qi, nq, lambda p: d_send.at[p], d_recv, 6)
+
+    def remote(src, dst, x, s_at, r_at, axis, peer):
+        return pltpu.make_async_remote_copy(
+            src_ref=src,
+            dst_ref=dst,
+            send_sem=ssem.at[x, s_at],
+            recv_sem=rsem.at[x, r_at],
+            device_id={axis: peer},
+            device_id_type=MESH,
+        )
+
+    def other_chips(act):
+        def step(off, _):
+            act(lax.rem(chip + off, nchip))
+            return 0
+
+        lax.fori_loop(1, nchip, step, 0)
+
+    own_slot, twin_base = core * nchip + chip, (1 - core) * nchip
+
+    def row_out(ch):
+        return remote(rows_ref, keys_i.at[own_slot], 0, ch, own_slot, "query", ch * 2 + core)
+
+    def row_twin():
+        return remote(rows_ref, keys_i.at[own_slot], 7, chip, own_slot, "query", twin)
+
+    def row_pass(ch):
+        at = core * nchip + ch
+        return remote(keys_i.at[at], keys_i.at[at], 7, ch, at, "query", twin)
+
+    def row_from_twin(ch):
+        at = twin_base + ch
+        return remote(keys_i.at[at], keys_i.at[at], 7, ch, at, "query", twin)
+
     barrier = pltpu.get_barrier_semaphore()
 
     def greet(axis, me, n):
@@ -139,8 +181,26 @@
 
     greet("query", qi, nq)
     greet("item", ii, ni)
-
-    lane = iota((8, dest), 1)
+    loads = [
+        pltpu.make_async_copy(a, b, in_sem.at[j])
+        for j, (a, b) in enumerate(
+            (
+                (rows_hbm, rows_ref),
+                (lists_hbm, lists_ref),
+                (counts_hbm, counts_ref),
+                (pos_hbm, pos_ref),
+                (table_hbm, table_v),
+                (q_hbm, q_ref),
+            )
+        )
+    ]
+    for load in loads:
+        load.start()
+    for load in loads[:4]:
+        load.wait()
+    keys_i[own_slot] = rows_ref[...]
+
+    lane = iota((1, dest), 1)
     lane_c, lane_r = lane // per, lane % per
     lane_key = lane_r
     for c in range(cap):
@@ -159,15 +219,15 @@
         both = jnp.concatenate([one * 256.0, one], axis=0).astype(BF16)
         found = jnp.dot(by_row, both, preferred_element_type=F32)
         found = jnp.where(iota((block, sl), 0) == (p & (block - 1)), found, 0.0)
-        cnt_send[s] = jnp.broadcast_to(jnp.sum(found, axis=0, keepdims=True), (8, sl))
+        cnt_send[s] = jnp.sum(found, axis=0, keepdims=True)
         return 0
 
     lax.fori_loop(0, ni, count_slice, 0)
     cnt_recv[ii] = cnt_send[ii]
-    keys_i[qi] = rows_ref[...]
 
     pl.semaphore_wait(barrier, nq + ni - 2)
-    x_row.start()
+    row_twin().start()
+    other_chips(lambda ch: row_out(ch).start())
     x_cnt.start()
     x_key.start()
 
@@ -179,7 +239,7 @@
     for c in range(cap):
         col = jnp.broadcast_to(cols[:, c : c + 1], (block, 128))
         lc_s[:, c * per : (c + 1) * per, :] = col.reshape(nq, per, 128)
-    table_in.wait()
+    loads[4].wait()
     pair = max(1, 16 // per)
     for c in range(0, cap, pair):
         parts = [
@@ -255,6 +315,7 @@
 
         lax.fori_loop(0, ntile, step, 0)
 
+    loads[5].wait()
     scores(keys_s, lc_s, e_s, mx_s, sm_s)
 
     x_cnt.wait_recv()
@@ -265,28 +326,53 @@
     log_send[...] = mine_logc
     log_recv[qi] = mine_logc
     x_log.start()
-    query_grads(keys_s, e_s, g_s)
+
+    def pass_on(ch):
+        remote(
+            keys_i.at[core * nchip + ch],
+            keys_i.at[core * nchip + ch],
+            0,
+            ch,
+            core * nchip + ch,
+            "query",
+            ch * 2 + core,
+        ).wait_recv()
+        row_pass(ch).start()
+
+    other_chips(pass_on)
+
+    x_key.wait_recv()
+    for g in range(nq):
+        want = iota((nblk * per, dest), 0)
+        hot[:, g * dest : (g + 1) * dest] = jnp.where(
+            want == key_recv[g], 1.0, 0.0
+        ).astype(BF16)
 
     x_log.wait_recv()
     for g in range(nq):
-        tp[g : g + 1, :] = log_recv[g, 0:1, :] * LOG2E
+        tp[g : g + 1, :] = log_recv[g] * LOG2E
     cols = jnp.transpose(tp[...])
     for g in range(nq):
-        lc_i[g] = jnp.broadcast_to(cols[:, g : g + 1], (sl, 128))
-    x_row.wait_recv()
+        lc_i[(g % 2) * nchip + g // 2] = jnp.broadcast_to(cols[:, g : g + 1], (sl, 128))
+
+    def from_twin(ch, _):
+        row_from_twin(ch).wait_recv()
+        return 0
+
+    lax.fori_loop(0, nchip, from_twin, 0)
     scores(keys_i, lc_i, e_i, mx_i, sm_i)
 
-    row8 = iota((8, sl), 0)
+    row2 = iota((2, sl), 0)
     for o in range(ni):
         at = slice(o * sl, (o + 1) * sl)
         top = jnp.maximum(mx_s[:, at], mx_i[:, at])
         part = sm_s[:, at] * jnp.exp2(mx_s[:, at] - top) + sm_i[:, at] * jnp.exp2(
             mx_i[:, at] - top
         )
-        stat_send[o] = jnp.where(row8 == 0, top, part)
+        stat_send[o] = jnp.where(row2 == 0, top, part)
     stat_recv[ii] = stat_send[ii]
     x_stat.start()
-    query_grads(keys_i, e_i, g_i)
+    query_grads(keys_s, e_s, g_s)
     x_stat.wait_recv()
     top = stat_recv[0, 0:1, :]
     for o in range(1, ni):
@@ -295,9 +381,10 @@
     for o in range(ni):
         part = part + stat_recv[o, 1:2, :] * jnp.exp2(stat_recv[o, 0:1, :] - top)
     lse2 = top + jnp.log(part) * LOG2E
-    lse_send[...] = jnp.broadcast_to(lse2, (8, sl))
-    lse_recv[ii] = lse_send[...]
+    lse_send[...] = lse2
+    lse_recv[ii] = lse2
     x_lse.start()
+    query_grads(keys_i, e_i, g_i)
 
     mine = pl.ds(pl.multiple_of(ii * sl, sl), sl)
     q_mine = q_ref[mine, :].astype(F32)
@@ -306,19 +393,12 @@
     label = jnp.sum(
         jnp.where(iota((sl, sl), 0) == iota((sl, sl), 1), label, 0.0), axis=0, keepdims=True
     )
-    loss_ref[...] = lse2 * LN2 - (label - mine_logc[0:1, :])
-
-    x_key.wait_recv()
-    for g in range(nq):
-        want = iota((nblk * per, dest), 0)
-        hot[:, g * dest : (g + 1) * dest] = jnp.where(
-            want == key_recv[g, 0:1, :], 1.0, 0.0
-        ).astype(BF16)
+    loss_ref[...] = lse2 * LN2 - (label - mine_logc)
 
     x_lse.wait_recv()
     for o in range(ni):
         at = slice(o * sl, (o + 1) * sl)
-        lse = lse_recv[o, 0:1, :]
+        lse = lse_recv[o]
         tp[o : o + 1, :] = jnp.exp2(mx_s[:, at] - lse) * SCALE
         tp[ni + o : ni + o + 1, :] = jnp.exp2(mx_i[:, at] - lse) * SCALE
     cols = jnp.transpose(tp[...])
@@ -328,53 +408,149 @@
         q = q_ref[at, :].astype(F32)
         wq_s[at, :] = (q * w_s).astype(BF16)
         wq_i[at, :] = (q * w_i).astype(BF16)
-        b_send[o] = (g_s[at, :] * w_s + g_i[at, :] * w_i).astype(BF16)
-    x_b.start()
-
-    def key_grads(e, wq, out, start, me):
-        n, rows = out.shape[0], out.shape[1]
+        g_s[at, :] = g_s[at, :] * w_s + g_i[at, :] * w_i
+
+    def own_part(zz, h):
+        at = pl.multiple_of((zz * 2 + h) * sl, sl)
+        return g_s[pl.ds(at, sl), :]
+
+    def ring_copy(way, hop, h):
+        to_z = lax.rem(z + (1 if way == 0 else nz - 1), nz)
+        return pltpu.make_async_remote_copy(
+            src_ref=ring_send.at[way, hop, h],
+            dst_ref=ring_recv.at[way, hop, h],
+            send_sem=ring_ssem.at[way, hop, h],
+            recv_sem=ring_rsem.at[way, hop, h],
+            device_id={"item": to_z * 2 + xh},
+            device_id_type=MESH,
+        )
+
+    def travels(way, hop, h):
+        return hop > 0 or h == way
+
+    def ring_hop(hop):
+        far = reach - hop
+        for h in range(2):
+            for way in range(2):
+                if not travels(way, hop, h):
+                    continue
+                at = lax.rem(z + (far if way == 0 else nz - far), nz)
+                val = own_part(at, h)
+                if hop > 0 and travels(way, hop - 1, h):
+                    ring_copy(way, hop - 1, h).wait_recv()
+                    val = val + ring_recv[way, hop - 1, h].astype(F32)
+                ring_send[way, hop, h] = val.astype(BF16)
+                ring_copy(way, hop, h).start()
+
+    def key_steps(e, wq, base, n, rows, use):
         step = max(1, min(n, KG // rows))
 
         def one(j, _):
-            at = pl.ds(pl.multiple_of(j * step * rows, step * rows), step * rows)
+            first = base + j * step
+            at = pl.ds(pl.multiple_of(first * rows, rows), step * rows)
             k = jnp.dot(e[at, :], wq[...], preferred_element_type=F32)
-            k = k.astype(BF16).reshape(step, rows, width)
-            for h in range(step):
-                p = j * step + h
-                out[p] = k[h]
-
-                @pl.when(p != me)
-                def _():
-                    start(p)
-
+            use(j, step, k.reshape(step, rows, width))
             return 0
 
         lax.fori_loop(0, n // step, one, 0)
 
-    key_grads(e_s, wq_s, d_send, x_d.start_to, qi)
+    ring_hop(0)
+
+    def send_rows(j, step, k):
+        k = k.astype(BF16)
+        for h in range(step):
+            p = j * step + h
+            d_send[p] = k[h]
+
+            @pl.when(p != qi)
+            def _():
+                x_d.start_to(p)
+
+    key_steps(e_s, wq_s, 0, nq, dest, send_rows)
     d_recv[qi] = d_send[qi]
-    key_grads(e_i, wq_i, c_send, x_c.start_to, qi)
-    c_recv[qi] = c_send[qi]
-    b_recv[ii] = b_send[ii]
-
-    def added(ref, n):
-        def step(o, acc):
-            return acc + ref[o].astype(F32)
-
-        return lax.fori_loop(0, n, step, jnp.zeros((sl, width), F32))
-
-    x_b.wait_recv()
-    qg_ref[...] = (added(b_recv, ni) - SCALE * r_mine).astype(BF16)
+    if reach > 1:
+        ring_hop(1)
+
+    def core_copy(ch):
+        return remote(core_send.at[ch], core_recv.at[ch], 8, ch, ch, "query", twin)
+
+    def send_twin(j, step, k):
+        k = k.astype(BF16)
+        for h in range(step):
+            ch = j * step + h
+            core_send[ch] = k[h]
+            core_copy(ch).start()
+
+    def c_copy(ch, slot):
+        return remote(c_send.at[ch], c_recv.at[slot], 9, ch, slot, "query", ch * 2 + core)
+
+    def send_chip(j, step, k):
+        for h in range(step):
+            ch = j * step + h
+            core_copy(ch).wait_recv()
+            c_send[ch] = (k[h] + core_recv[ch].astype(F32)).astype(BF16)
+
+            @pl.when(ch != chip)
+            def _():
+                c_copy(ch, chip).start()
+
+    key_steps(e_i, wq_i, twin_base, nchip, sl, send_twin)
+    if reach > 2:
+        ring_hop(2)
+    key_steps(e_i, wq_i, core * nchip, nchip, sl, send_chip)
+    c_recv[chip] = c_send[chip]
+    for hop in range(3, reach):
+        ring_hop(hop)
+
+    sums = []
+    for h in range(2):
+        val = own_part(z, h)
+        for way in range(2):
+            if travels(way, reach - 1, h):
+                ring_copy(way, reach - 1, h).wait_recv()
+                val = val + ring_recv[way, reach - 1, h].astype(F32)
+        sums.append(val)
+    half_send[...] = jnp.where(xh == 0, sums[1], sums[0]).astype(BF16)
+    half = remote(half_send, half_recv, 10, 0, 0, "item", mirror)
+    half.start()
+    mine_sum = jnp.where(xh == 0, sums[0], sums[1])
+    half.wait_recv()
+    qg_ref[...] = (mine_sum + half_recv[...].astype(F32) - SCALE * r_mine).astype(BF16)
+
     x_d.wait_recv()
     grads = jnp.dot(
         hot[...], d_recv[...].reshape(nq * dest, width), preferred_element_type=F32
     )
     tg_ref[...] = grads.reshape(nblk, per, width).astype(BF16)
-    x_c.wait_recv()
-    pg_ref[...] = (added(c_recv, nq) - SCALE * q_mine).astype(BF16)
-
-    for x in (x_row, x_cnt, x_log, x_key, x_stat, x_lse, x_b, x_c, x_d):
+
+    other_chips(lambda ch: c_copy(ch, ch).wait_recv())
+    total = c_recv[0].astype(F32)
+    for ch in range(1, nchip):
+        total = total + c_recv[ch].astype(F32)
+    pg_ref[...] = (total - SCALE * q_mine).astype(BF16)
+
+    for x in (x_cnt, x_log, x_key, x_stat, x_lse, x_d):
         x.wait_send()
+    row_twin().wait_send()
+    half.wait_send()
+    for hop in range(reach):
+        for h in range(2):
+            for way in range(2):
+                if travels(way, hop, h):
+                    ring_copy(way, hop, h).wait_send()
+
+    def sent(ch):
+        row_out(ch).wait_send()
+        row_pass(ch).wait_send()
+        c_copy(ch, chip).wait_send()
+
+    other_chips(sent)
+
+    def sent_twin(ch, _):
+        core_copy(ch).wait_send()
+        return 0
+
+    lax.fori_loop(0, nchip, sent_twin, 0)
 
 
 def solution(mesh):
@@ -387,6 +563,7 @@
         dest = cap * per
         nk_s, nk_i = nq * dest, nq * sl
         most = max(nk_s, nk_i)
+        reach = ni // 4
         vm, dma = pltpu.VMEM, pltpu.SemaphoreType.DMA
         whole = pl.BlockSpec(memory_space=vm)
         loss, qg, pg, tg = pl.pallas_call(
@@ -397,17 +574,15 @@
                 jax.ShapeDtypeStruct((sl, width), BF16),
                 jax.ShapeDtypeStruct((nblk, per, width), BF16),
             ),
-            in_specs=[
-                pl.BlockSpec(memory_space=pl.ANY),
-                whole,
-                whole,
-                pl.BlockSpec(memory_space=pltpu.SMEM),
-                whole,
-                whole,
-            ],
+            in_specs=[pl.BlockSpec(memory_space=pl.ANY)] * 6,
             out_specs=[whole] * 4,
             scratch_shapes=[
                 vm((nblk, block, width), BF16),
+                vm((nqry, width), BF16),
+                vm((nblk, block), I32),
+                pltpu.SMEM((1, 1, cap), I32),
+                vm((ni, 128), I32),
+                vm((sl, width), BF16),
                 vm((nq, dest, width), BF16),
                 vm((nq, sl, width), BF16),
                 vm((nq, dest, 128), F32),
@@ -427,26 +602,32 @@
                 vm((nqry, width), BF16),
                 vm((nqry, width), BF16),
                 vm((128, 128), F32),
-                vm((ni, 8, sl), F32),
-                vm((ni, 8, sl), F32),
-                vm((8, sl), F32),
-                vm((nq, 8, sl), F32),
-                vm((8, dest), I32),
-                vm((nq, 8, dest), I32),
-                vm((ni, 8, sl), F32),
-                vm((ni, 8, sl), F32),
-                vm((8, sl), F32),
-                vm((ni, 8, sl), F32),
-                vm((ni, sl, width), BF16),
-                vm((ni, sl, width), BF16),
-                vm((nq, sl, width), BF16),
-                vm((nq, sl, width), BF16),
+                vm((ni, 1, sl), F32),
+                vm((ni, 1, sl), F32),
+                vm((1, sl), F32),
+                vm((nq, 1, sl), F32),
+                vm((1, dest), I32),
+                vm((nq, 1, dest), I32),
+                vm((ni, 2, sl), F32),
+                vm((ni, 2, sl), F32),
+                vm((1, sl), F32),
+                vm((ni, 1, sl), F32),
+                vm((2, reach, 2, sl, width), BF16),
+                vm((2, reach, 2, sl, width), BF16),
+                vm((sl, width), BF16),
+                vm((sl, width), BF16),
+                vm((nq // 2, sl, width), BF16),
+                vm((nq // 2, sl, width), BF16),
+                vm((nq // 2, sl, width), BF16),
+                vm((nq // 2, sl, width), BF16),
                 vm((nq, dest, width), BF16),
                 vm((nq, dest, width), BF16),
                 vm((nblk * per, nq * dest), BF16),
-                dma,
-                dma((9, max(nq, ni))),
-                dma((9, max(nq, ni))),
+                dma((6,)),
+                dma((11, max(nq, ni))),
+                dma((11, max(nq, ni))),
+                dma((2, reach, 2)),
+                dma((2, reach, 2)),
             ],
             compiler_params=pltpu.CompilerParams(
                 collective_id=0, has_side_effects=True, vmem_limit_bytes=60 << 20

time: 96.9 us -> 74.5 us (0.77)
  the two profiles are of different devices: /device:TPU:29 before, /device:TPU:32 now
where the time goes in v2:
time: 74.5 us; the launch traced here: 74.3 us
  Pallas kernels  68 us (91%)
  local copies, waits for them, and re-layouts  5.73 us (8%)
    pallas_call x1, Pallas kernels, step(): pl.pallas_call(functools.partial(kernel, nq, ni), out_shape=(jax.ShapeDty...  68 us
    unnamed x4, local copies, waits for them, and re-layouts  5.73 us

profile of v2, /device:TPU:32, one launch (start us, length us, event | category | flops | bytes accessed | tf_op | source)
XLA Modules:
  0.0 74.3 jit_solution(1261575844745647811)
XLA Ops:
  0.6 68.0 %shard_map.93 = (f32[1,128]{1,0:T(1,128)}, bf16[128,256]{1,0:T(8,128)(2,1)}, bf16[128,256]{1,0:T(8,128)(2,1)}, bf16[64,8,256]{2,1,0:T(8,128)(2,1)}) custom-call(bf16[64,128,256]{2,1,0:T(8,128)(2,1)} %table_hbm.1, bf16[2048,256]{1,0:T(8,128)(2,1)} %q_hbm.1, s32[64,128]{1,0:T(8,128)} %counts_hbm.1, s32[1,1,16]{2,1,0:T(1,128)} %lists_hbm.1, s32[16,128]{1,0:T(8,128)} %bitcast.2, ...), custom_call_target="tpu_custom_call" | custom-call | tf_op jit(solution)/shard_map/pallas_call | solution.py:569
  68.6 1.1 %copy.14 = f32[128]{0:T(128)} copy(f32[128]{0:T(128)} %bitcast.3) | data formatting | bytes 1024
  69.7 1.5 %copy.15 = bf16[128,256]{1,0:T(8,128)(2,1)} copy(bf16[128,256]{1,0:T(8,128)(2,1)} %get-tuple-element.17) | data formatting | bytes 131072
  71.2 1.5 %copy.16 = bf16[128,256]{1,0:T(8,128)(2,1)} copy(bf16[128,256]{1,0:T(8,128)(2,1)} %get-tuple-element.18) | data formatting | bytes 131072
  72.7 1.7 %copy.17 = bf16[64,8,256]{2,1,0:T(8,128)(2,1)} copy(bf16[64,8,256]{2,1,0:T(8,128)(2,1)} %get-tuple-element.19) | data formatting | bytes 524288

commit v3 on v2

--- a/solution.py
+++ b/solution.py
@@ -65,14 +65,19 @@
     log_recv,
     key_send,
     key_recv,
+    row_mx,
+    row_sm,
     stat_send,
     stat_recv,
-    lse_send,
-    lse_recv,
+    pair_send,
+    pair_recv,
+    lse_rows,
     ring_send,
     ring_recv,
     half_send,
     half_recv,
+    half_mine,
+    tgrad,
     core_send,
     core_recv,
     c_send,
@@ -123,6 +128,7 @@
         class X:
             start_to = staticmethod(lambda p: copy(p, me).start())
             start = staticmethod(lambda: each(X.start_to))
+            wait_from = staticmethod(lambda p: copy(p, p).wait_recv())
             wait_recv = staticmethod(lambda: each(lambda p: copy(p, p).wait_recv()))
             wait_send = staticmethod(lambda: each(lambda p: copy(p, me).wait_send()))
 
@@ -131,8 +137,6 @@
     x_cnt = to("item", ii, ni, lambda p: cnt_send.at[p], cnt_recv, 1)
     x_log = to("query", qi, nq, lambda p: log_send, log_recv, 2)
     x_key = to("query", qi, nq, lambda p: key_send, key_recv, 3)
-    x_stat = to("item", ii, ni, lambda p: stat_send.at[p], stat_recv, 4)
-    x_lse = to("item", ii, ni, lambda p: lse_send, lse_recv, 5)
     x_d = to("query", qi, nq, lambda p: d_send.at[p], d_recv, 6)
 
     def remote(src, dst, x, s_at, r_at, axis, peer):
@@ -196,9 +200,31 @@
     ]
     for load in loads:
         load.start()
-    for load in loads[:4]:
+    loads[0].wait()
+    keys_i[own_slot] = rows_ref[...]
+    pl.semaphore_wait(barrier, nq + ni - 2)
+    other_chips(lambda ch: row_out(ch).start())
+    row_twin().start()
+    for load in loads[1:4]:
         load.wait()
-    keys_i[own_slot] = rows_ref[...]
+
+    cnt = counts_ref[...]
+    halves = jnp.concatenate([cnt >> 8, cnt & 255], axis=0).astype(F32)
+    by_row = jnp.transpose(halves).astype(BF16)
+
+    wide = min(4, ni)
+    for o in range(0, ni, wide):
+        p = jnp.concatenate([pos_ref[o + j : o + j + 1, :] for j in range(wide)], axis=1)
+        blk = (p >> 7) - ii * nblk
+        one = (iota((nblk, wide * sl), 0) == blk).astype(F32)
+        both = jnp.concatenate([one * 256.0, one], axis=0).astype(BF16)
+        found = jnp.dot(by_row, both, preferred_element_type=F32)
+        found = jnp.where(iota((block, wide * sl), 0) == (p & (block - 1)), found, 0.0)
+        found = jnp.sum(found, axis=0, keepdims=True)
+        for j in range(wide):
+            cnt_send[o + j] = found[:, j * sl : (j + 1) * sl]
+    cnt_recv[ii] = cnt_send[ii]
+    x_cnt.start()
 
     lane = iota((1, dest), 1)
     lane_c, lane_r = lane // per, lane % per
@@ -207,28 +233,6 @@
         lane_key = lane_key + jnp.where(lane_c == c, lists_ref[0, 0, c] * per, 0)
     key_send[...] = lane_key
     key_recv[qi] = lane_key
-
-    cnt = counts_ref[...]
-    halves = jnp.concatenate([cnt >> 8, cnt & 255], axis=0).astype(F32)
-    by_row = jnp.transpose(halves).astype(BF16)
-
-    def count_slice(s, _):
-        p = pos_ref[pl.ds(s, 1), :]
-        blk = (p >> 7) - ii * nblk
-        one = (iota((nblk, sl), 0) == blk).astype(F32)
-        both = jnp.concatenate([one * 256.0, one], axis=0).astype(BF16)
-        found = jnp.dot(by_row, both, preferred_element_type=F32)
-        found = jnp.where(iota((block, sl), 0) == (p & (block - 1)), found, 0.0)
-        cnt_send[s] = jnp.sum(found, axis=0, keepdims=True)
-        return 0
-
-    lax.fori_loop(0, ni, count_slice, 0)
-    cnt_recv[ii] = cnt_send[ii]
-
-    pl.semaphore_wait(barrier, nq + ni - 2)
-    row_twin().start()
-    other_chips(lambda ch: row_out(ch).start())
-    x_cnt.start()
     x_key.start()
 
     tp[...] = jnp.zeros_like(tp)
@@ -254,7 +258,7 @@
         step = max(1, min(n, size // rows))
         return [(j, j + step) for j in range(0, n, step)], rows
 
-    def scores(keys, lc, e, mx, sm):
+    def scores(keys, lc, e, mx, sm, between=None):
         spans, rows = chunks(keys, KC)
 
         def tile_of(t):
@@ -297,35 +301,34 @@
             return 0
 
         lax.fori_loop(0, ntile // 2 - 1, pair_of_tiles, 0)
+        if between is not None:
+            between()
         both(ntile - 1, s_b, m_b, ntile - 2, s_a, m_a)
         both(None, None, None, ntile - 1, s_b, m_b)
 
-    def query_grads(keys, e, g):
+    def query_grads(keys, e, g, half):
         n = keys.shape[0] * keys.shape[1]
-
-        def step(t, _):
-            at = pl.ds(pl.multiple_of(t * TQ, TQ), TQ)
-            g[at, :] = lax.dot_general(
-                e[:, at],
-                keys[...].reshape(n, width),
-                (((0,), (0,)), ((), ())),
-                preferred_element_type=F32,
-            )
-            return 0
-
-        lax.fori_loop(0, ntile, step, 0)
+        at = slice(half * nqry // 2, (half + 1) * nqry // 2)
+        g[at, :] = lax.dot_general(
+            e[:, at],
+            keys[...].reshape(n, width),
+            (((0,), (0,)), ((), ())),
+            preferred_element_type=F32,
+        )
 
     loads[5].wait()
-    scores(keys_s, lc_s, e_s, mx_s, sm_s)
-
-    x_cnt.wait_recv()
-    total = cnt_recv[0]
-    for o in range(1, ni):
-        total = total + cnt_recv[o]
-    mine_logc = jnp.log(total).astype(BF16).astype(F32)
-    log_send[...] = mine_logc
-    log_recv[qi] = mine_logc
-    x_log.start()
+
+    def log_counts():
+        x_cnt.wait_recv()
+        total = cnt_recv[0]
+        for o in range(1, ni):
+            total = total + cnt_recv[o]
+        mine_logc = jnp.log(total).astype(BF16).astype(F32)
+        log_send[...] = mine_logc
+        log_recv[qi] = mine_logc
+        x_log.start()
+
+    scores(keys_s, lc_s, e_s, mx_s, sm_s, log_counts)
 
     def pass_on(ch):
         remote(
@@ -348,6 +351,7 @@
             want == key_recv[g], 1.0, 0.0
         ).astype(BF16)
 
+    query_grads(keys_s, e_s, g_s, 0)
     x_log.wait_recv()
     for g in range(nq):
         tp[g : g + 1, :] = log_recv[g] * LOG2E
@@ -362,29 +366,47 @@
     lax.fori_loop(0, nchip, from_twin, 0)
     scores(keys_i, lc_i, e_i, mx_i, sm_i)
 
-    row2 = iota((2, sl), 0)
     for o in range(ni):
         at = slice(o * sl, (o + 1) * sl)
-        top = jnp.maximum(mx_s[:, at], mx_i[:, at])
-        part = sm_s[:, at] * jnp.exp2(mx_s[:, at] - top) + sm_i[:, at] * jnp.exp2(
-            mx_i[:, at] - top
-        )
-        stat_send[o] = jnp.where(row2 == 0, top, part)
-    stat_recv[ii] = stat_send[ii]
-    x_stat.start()
-    query_grads(keys_s, e_s, g_s)
-    x_stat.wait_recv()
-    top = stat_recv[0, 0:1, :]
-    for o in range(1, ni):
-        top = jnp.maximum(top, stat_recv[o, 0:1, :])
-    part = jnp.zeros((1, sl), F32)
-    for o in range(ni):
-        part = part + stat_recv[o, 1:2, :] * jnp.exp2(stat_recv[o, 0:1, :] - top)
-    lse2 = top + jnp.log(part) * LOG2E
-    lse_send[...] = lse2
-    lse_recv[ii] = lse2
-    x_lse.start()
-    query_grads(keys_i, e_i, g_i)
+        row_mx[o : o + 1, :] = mx_s[:, at]
+        row_mx[ni + o : ni + o + 1, :] = mx_i[:, at]
+        row_sm[o : o + 1, :] = sm_s[:, at]
+        row_sm[ni + o : ni + o + 1, :] = sm_i[:, at]
+
+    def met(pairs):
+        top = pairs[0][0]
+        for m, _ in pairs[1:]:
+            top = jnp.maximum(top, m)
+        return top, sum(v * jnp.exp2(m - top) for m, v in pairs)
+
+    top, part = met(
+        [(row_mx[j : j + ni, :], row_sm[j : j + ni, :]) for j in (0, ni)]
+    )
+    stat_send[0], stat_send[1] = top, part
+    stat_recv[z, 0], stat_recv[z, 1] = top, part
+
+    def stat_copy(zz, slot):
+        return remote(stat_send, stat_recv.at[slot], 4, zz, slot, "item", zz * 2 + xh)
+
+    def other_z(act):
+        def step(off, _):
+            act(lax.rem(z + off, nz))
+            return 0
+
+        lax.fori_loop(1, nz, step, 0)
+
+    other_z(lambda zz: stat_copy(zz, z).start())
+    query_grads(keys_s, e_s, g_s, 1)
+    other_z(lambda zz: stat_copy(zz, zz).wait_recv())
+    top, part = met([(stat_recv[j, 0], stat_recv[j, 1]) for j in range(nz)])
+    pair_send[0], pair_send[1] = top, part
+    stat_pair = remote(pair_send, pair_recv, 5, 0, 0, "item", mirror)
+    stat_pair.start()
+    query_grads(keys_i, e_i, g_i, 0)
+    query_grads(keys_i, e_i, g_i, 1)
+    stat_pair.wait_recv()
+    top, part = met([(pair_send[0], pair_send[1]), (pair_recv[0], pair_recv[1])])
+    lse_rows[...] = top + jnp.log(part) * LOG2E
 
     mine = pl.ds(pl.multiple_of(ii * sl, sl), sl)
     q_mine = q_ref[mine, :].astype(F32)
@@ -393,14 +415,10 @@
     label = jnp.sum(
         jnp.where(iota((sl, sl), 0) == iota((sl, sl), 1), label, 0.0), axis=0, keepdims=True
     )
-    loss_ref[...] = lse2 * LN2 - (label - mine_logc)
-
-    x_lse.wait_recv()
-    for o in range(ni):
-        at = slice(o * sl, (o + 1) * sl)
-        lse = lse_recv[o]
-        tp[o : o + 1, :] = jnp.exp2(mx_s[:, at] - lse) * SCALE
-        tp[ni + o : ni + o + 1, :] = jnp.exp2(mx_i[:, at] - lse) * SCALE
+    loss_ref[...] = lse_rows[pl.ds(ii, 1), :] * LN2 - (label - log_send[...])
+
+    for j in (0, ni):
+        tp[j : j + ni, :] = jnp.exp2(row_mx[j : j + ni, :] - lse_rows[...]) * SCALE
     cols = jnp.transpose(tp[...])
     for o in range(ni):
         at = slice(o * sl, (o + 1) * sl)
@@ -428,24 +446,29 @@
     def travels(way, hop, h):
         return hop > 0 or h == way
 
-    def ring_hop(hop):
+    def ring_step(late, hop):
         far = reach - hop
-        for h in range(2):
-            for way in range(2):
-                if not travels(way, hop, h):
-                    continue
-                at = lax.rem(z + (far if way == 0 else nz - far), nz)
-                val = own_part(at, h)
-                if hop > 0 and travels(way, hop - 1, h):
-                    ring_copy(way, hop - 1, h).wait_recv()
-                    val = val + ring_recv[way, hop - 1, h].astype(F32)
-                ring_send[way, hop, h] = val.astype(BF16)
-                ring_copy(way, hop, h).start()
-
-    def key_steps(e, wq, base, n, rows, use):
+        for way in range(2):
+            h = way if late == 0 else 1 - way
+            at = lax.rem(z + (far if way == 0 else nz - far), nz)
+            val = own_part(at, h)
+            if hop > late:
+                ring_copy(way, hop - 1, h).wait_recv()
+                val = val + ring_recv[way, hop - 1, h].astype(F32)
+            ring_send[way, hop, h] = val.astype(BF16)
+            ring_copy(way, hop, h).start()
+
+    ring_steps = [(late, hop) for hop in range(1, reach) for late in (1, 0) if hop > late]
+
+    def ring_next():
+        if ring_steps:
+            ring_step(*ring_steps.pop(0))
+
+    def key_steps(e, wq, base, n, rows, use, shift=0):
         step = max(1, min(n, KG // rows))
 
         def one(j, _):
+            j = lax.rem(j + shift, n // step)
             first = base + j * step
             at = pl.ds(pl.multiple_of(first * rows, rows), step * rows)
             k = jnp.dot(e[at, :], wq[...], preferred_element_type=F32)
@@ -454,7 +477,9 @@
 
         lax.fori_loop(0, n // step, one, 0)
 
-    ring_hop(0)
+    ring_step(0, 0)
+    if reach > 1:
+        ring_step(1, 1)
 
     def send_rows(j, step, k):
         k = k.astype(BF16)
@@ -466,10 +491,11 @@
             def _():
                 x_d.start_to(p)
 
-    key_steps(e_s, wq_s, 0, nq, dest, send_rows)
+    lines = 4 if nq >= 16 else 1
+    line = qi // (nq // lines)
+    key_steps(e_s, wq_s, 0, nq, dest, send_rows, line + 2)
     d_recv[qi] = d_send[qi]
-    if reach > 1:
-        ring_hop(1)
+    ring_next()
 
     def core_copy(ch):
         return remote(core_send.at[ch], core_recv.at[ch], 8, ch, ch, "query", twin)
@@ -495,13 +521,36 @@
                 c_copy(ch, chip).start()
 
     key_steps(e_i, wq_i, twin_base, nchip, sl, send_twin)
-    if reach > 2:
-        ring_hop(2)
+    ring_next()
     key_steps(e_i, wq_i, core * nchip, nchip, sl, send_chip)
     c_recv[chip] = c_send[chip]
-    for hop in range(3, reach):
-        ring_hop(hop)
-
+    while ring_steps:
+        ring_next()
+
+    def table_part(j):
+        many = nq // lines
+        first = lax.rem(line + j, lines) * many
+
+        def arrived(k, _):
+            @pl.when(first + k != qi)
+            def _():
+                x_d.wait_from(first + k)
+
+            return 0
+
+        lax.fori_loop(0, many, arrived, 0)
+        at = pl.ds(pl.multiple_of(first * dest, dest), many * dest)
+        got = d_recv[pl.ds(first, many)].reshape(many * dest, width)
+        part = jnp.dot(hot[:, at], got, preferred_element_type=F32)
+        if j > 0:
+            part = part + tgrad[...]
+        if j < lines - 1:
+            tgrad[...] = part
+        else:
+            tg_ref[...] = part.reshape(nblk, per, width).astype(BF16)
+
+    for j in range(lines // 2):
+        table_part(j)
     sums = []
     for h in range(2):
         val = own_part(z, h)
@@ -513,15 +562,11 @@
     half_send[...] = jnp.where(xh == 0, sums[1], sums[0]).astype(BF16)
     half = remote(half_send, half_recv, 10, 0, 0, "item", mirror)
     half.start()
-    mine_sum = jnp.where(xh == 0, sums[0], sums[1])
+    half_mine[...] = jnp.where(xh == 0, sums[0], sums[1]) - SCALE * r_mine
+    for j in range(lines // 2, lines):
+        table_part(j)
     half.wait_recv()
-    qg_ref[...] = (mine_sum + half_recv[...].astype(F32) - SCALE * r_mine).astype(BF16)
-
-    x_d.wait_recv()
-    grads = jnp.dot(
-        hot[...], d_recv[...].reshape(nq * dest, width), preferred_element_type=F32
-    )
-    tg_ref[...] = grads.reshape(nblk, per, width).astype(BF16)
+    qg_ref[...] = (half_mine[...] + half_recv[...].astype(F32)).astype(BF16)
 
     other_chips(lambda ch: c_copy(ch, ch).wait_recv())
     total = c_recv[0].astype(F32)
@@ -529,9 +574,11 @@
         total = total + c_recv[ch].astype(F32)
     pg_ref[...] = (total - SCALE * q_mine).astype(BF16)
 
-    for x in (x_cnt, x_log, x_key, x_stat, x_lse, x_d):
+    for x in (x_cnt, x_log, x_key, x_d):
         x.wait_send()
     row_twin().wait_send()
+    other_z(lambda zz: stat_copy(zz, z).wait_send())
+    stat_pair.wait_send()
     half.wait_send()
     for hop in range(reach):
         for h in range(2):
@@ -551,6 +598,11 @@
         return 0
 
     lax.fori_loop(0, nchip, sent_twin, 0)
+
+
+def hand_over(*refs):
+    for j in range(4):
+        refs[4 + j][...] = refs[j][...]
 
 
 def solution(mesh):
@@ -608,14 +660,19 @@
                 vm((nq, 1, sl), F32),
                 vm((1, dest), I32),
                 vm((nq, 1, dest), I32),
-                vm((ni, 2, sl), F32),
-                vm((ni, 2, sl), F32),
-                vm((1, sl), F32),
-                vm((ni, 1, sl), F32),
+                vm((2 * ni, sl), F32),
+                vm((2 * ni, sl), F32),
+                vm((2, ni, sl), F32),
+                vm((ni // 2, 2, ni, sl), F32),
+                vm((2, ni, sl), F32),
+                vm((2, ni, sl), F32),
+                vm((ni, sl), F32),
                 vm((2, reach, 2, sl, width), BF16),
                 vm((2, reach, 2, sl, width), BF16),
                 vm((sl, width), BF16),
                 vm((sl, width), BF16),
+                vm((sl, width), F32),
+                vm((nblk * per, width), F32),
                 vm((nq // 2, sl, width), BF16),
                 vm((nq // 2, sl, width), BF16),
                 vm((nq // 2, sl, width), BF16),
@@ -633,6 +690,11 @@
                 collective_id=0, has_side_effects=True, vmem_limit_bytes=60 << 20
             ),
         )(table, queries, counts, lists, positives.reshape(-1, 128), positive_rows)
+        parts = (loss, qg, pg, tg)
+        loss, qg, pg, tg = pl.pallas_call(
+            hand_over,
+            out_shape=tuple(jax.ShapeDtypeStruct(a.shape, a.dtype) for a in parts),
+        )(*parts)
         return loss.reshape(sl), qg, pg, tg
 
     return jax.shard_map(

time: 74.5 us -> 65.4 us (0.88)
  local copies, waits for them, and re-layouts: 5.73 us -> 0 us
  Pallas kernels: 68 us -> 64.7 us
    unnamed x4 -> x0, local copies, waits for them, and re-layouts: 5.73 us -> none
    pallas_call x1, Pallas kernels: 68 us -> 62.9 us  [step(): pl.pallas_call(functools.partial(kernel, nq, ni), out_shape=(jax.ShapeDty...]
    pallas_call x0 -> x1, Pallas kernels: none -> 1.79 us  [step(): pl.pallas_call(hand_over, out_shape=tuple((jax.ShapeDtypeStruct(a.shape,...]
where the time goes in v3:
time: 65.4 us; the launch traced here: 65.3 us
  Pallas kernels  64.7 us (99%)
    pallas_call x1, Pallas kernels, step(): pl.pallas_call(functools.partial(kernel, nq, ni), out_shape=(jax.ShapeDty...  62.9 us
    pallas_call x1, Pallas kernels, step(): pl.pallas_call(hand_over, out_shape=tuple((jax.ShapeDtypeStruct(a.shape,...  1.79 us

profile of v3, /device:TPU:32, one launch (start us, length us, event | category | flops | bytes accessed | tf_op | source)
XLA Modules:
  0.0 65.3 jit_solution(14721845559518383282)
XLA Ops:
  0.6 62.9 %shard_map.93 = (f32[1,128]{1,0:T(1,128)}, bf16[128,256]{1,0:T(8,128)(2,1)}, bf16[128,256]{1,0:T(8,128)(2,1)}, bf16[64,8,256]{2,1,0:T(8,128)(2,1)}) custom-call(bf16[64,128,256]{2,1,0:T(8,128)(2,1)} %table_hbm.1, bf16[2048,256]{1,0:T(8,128)(2,1)} %q_hbm.1, s32[64,128]{1,0:T(8,128)} %counts_hbm.1, s32[1,1,16]{2,1,0:T(1,128)} %lists_hbm.1, s32[16,128]{1,0:T(8,128)} %bitcast.2, ...), custom_call_target="tpu_custom_call" | custom-call | tf_op jit(solution)/shard_map/pallas_call | solution.py:621
  63.6 1.8 %shard_map.94 = (f32[1,128]{1,0:T(1,128)}, bf16[128,256]{1,0:T(8,128)(2,1)}, bf16[128,256]{1,0:T(8,128)(2,1)}, bf16[64,8,256]{2,1,0:T(8,128)(2,1)}) custom-call(f32[1,128]{1,0:T(1,128)} %get-tuple-element.12.refs_0_, bf16[128,256]{1,0:T(8,128)(2,1)} %get-tuple-element.13.refs_1_, bf16[128,256]{1,0:T(8,128)(2,1)} %get-tuple-element.14.refs_2_, ...), custom_call_target="tpu_custom_call" | custom-call | tf_op jit(solution)/shard_map/pallas_call | solution.py:694

commit v4 on v3

--- a/solution.py
+++ b/solution.py
@@ -621,10 +621,10 @@
         loss, qg, pg, tg = pl.pallas_call(
             functools.partial(kernel, nq, ni),
             out_shape=(
-                jax.ShapeDtypeStruct((1, sl), F32),
-                jax.ShapeDtypeStruct((sl, width), BF16),
-                jax.ShapeDtypeStruct((sl, width), BF16),
-                jax.ShapeDtypeStruct((nblk, per, width), BF16),
+                vm((1, sl), F32),
+                vm((sl, width), BF16),
+                vm((sl, width), BF16),
+                vm((nblk, per, width), BF16),
             ),
             in_specs=[pl.BlockSpec(memory_space=pl.ANY)] * 6,
             out_specs=[whole] * 4,
@@ -694,7 +694,9 @@
         loss, qg, pg, tg = pl.pallas_call(
             hand_over,
             out_shape=tuple(jax.ShapeDtypeStruct(a.shape, a.dtype) for a in parts),
-        )(*parts)
+            in_specs=[whole] * 4,
+            out_specs=[whole] * 4,
+        )(*(pltpu.with_memory_space_constraint(a, vm) for a in parts))
         return loss.reshape(sl), qg, pg, tg
 
     return jax.shard_map(

time: 65.4 us -> 63.7 us (0.974)
  Pallas kernels: 64.7 us -> 62.9 us
    pallas_call x1, Pallas kernels: 1.79 us -> 0.77 us  [step(): pl.pallas_call(hand_over, out_shape=tuple((jax.ShapeDtypeStruct(a.shape,...]
    pallas_call x1, Pallas kernels: 62.9 us -> 62.2 us  [step(): pl.pallas_call(functools.partial(kernel, nq, ni), out_shape=(vm((1, sl),...]
where the time goes in v4:
time: 63.7 us; the launch traced here: 63.6 us
  Pallas kernels  62.9 us (99%)
  between operations  0.64 us (1%)
    pallas_call x1, Pallas kernels, step(): pl.pallas_call(functools.partial(kernel, nq, ni), out_shape=(vm((1, sl),...  62.2 us

profile of v4, /device:TPU:32, one launch (start us, length us, event | category | flops | bytes accessed | tf_op | source)
XLA Modules:
  0.0 63.6 jit_solution(3336728232085047876)
XLA Ops:
  0.6 62.2 %shard_map.93 = (f32[1,128]{1,0:T(1,128)S(1)}, bf16[128,256]{1,0:T(8,128)(2,1)S(1)}, bf16[128,256]{1,0:T(8,128)(2,1)S(1)}, bf16[64,8,256]{2,1,0:T(8,128)(2,1)S(1)}) custom-call(bf16[64,128,256]{2,1,0:T(8,128)(2,1)} %table_hbm.1, bf16[2048,256]{1,0:T(8,128)(2,1)} %q_hbm.1, s32[64,128]{1,0:T(8,128)} %counts_hbm.1, s32[1,1,16]{2,1,0:T(1,128)} %lists_hbm.1, ...), custom_call_target="tpu_custom_call" | custom-call | tf_op jit(solution)/shard_map/pallas_call | solution.py:621
  62.8 0.8 %shard_map.94 = (f32[1,128]{1,0:T(1,128)}, bf16[128,256]{1,0:T(8,128)(2,1)}, bf16[128,256]{1,0:T(8,128)(2,1)}, bf16[64,8,256]{2,1,0:T(8,128)(2,1)}) custom-call(f32[1,128]{1,0:T(1,128)S(1)} %get-tuple-element.12.refs_0_, bf16[128,256]{1,0:T(8,128)(2,1)S(1)} %get-tuple-element.13.refs_1_, bf16[128,256]{1,0:T(8,128)(2,1)S(1)} %get-tuple-element.14.refs_2_, ...), custom_call_target="tpu_custom_call" | custom-call | tf_op jit(solution)/shard_map/pallas_call | solution.py:694

commit v5 on v4

--- a/solution.py
+++ b/solution.py
@@ -549,7 +549,7 @@
         else:
             tg_ref[...] = part.reshape(nblk, per, width).astype(BF16)
 
-    for j in range(lines // 2):
+    for j in range(lines // 4):
         table_part(j)
     sums = []
     for h in range(2):
@@ -563,7 +563,7 @@
     half = remote(half_send, half_recv, 10, 0, 0, "item", mirror)
     half.start()
     half_mine[...] = jnp.where(xh == 0, sums[0], sums[1]) - SCALE * r_mine
-    for j in range(lines // 2, lines):
+    for j in range(lines // 4, lines):
         table_part(j)
     half.wait_recv()
     qg_ref[...] = (half_mine[...] + half_recv[...].astype(F32)).astype(BF16)

time: 63.7 us -> 63.7 us (level)
  no operation moved by 1% of the time
where the time goes in v5:
time: 63.7 us; the launch traced here: 63.6 us
  Pallas kernels  62.9 us (99%)
  between operations  0.64 us (1%)
    pallas_call x1, Pallas kernels, step(): pl.pallas_call(functools.partial(kernel, nq, ni), out_shape=(vm((1, sl),...  62.2 us

profile of v5, /device:TPU:32, one launch (start us, length us, event | category | flops | bytes accessed | tf_op | source)
XLA Modules:
  0.0 63.6 jit_solution(9696928461953911786)
XLA Ops:
  0.6 62.2 %shard_map.93 = (f32[1,128]{1,0:T(1,128)S(1)}, bf16[128,256]{1,0:T(8,128)(2,1)S(1)}, bf16[128,256]{1,0:T(8,128)(2,1)S(1)}, bf16[64,8,256]{2,1,0:T(8,128)(2,1)S(1)}) custom-call(bf16[64,128,256]{2,1,0:T(8,128)(2,1)} %table_hbm.1, bf16[2048,256]{1,0:T(8,128)(2,1)} %q_hbm.1, s32[64,128]{1,0:T(8,128)} %counts_hbm.1, s32[1,1,16]{2,1,0:T(1,128)} %lists_hbm.1, ...), custom_call_target="tpu_custom_call" | custom-call | tf_op jit(solution)/shard_map/pallas_call | solution.py:621
  62.8 0.8 %shard_map.94 = (f32[1,128]{1,0:T(1,128)}, bf16[128,256]{1,0:T(8,128)(2,1)}, bf16[128,256]{1,0:T(8,128)(2,1)}, bf16[64,8,256]{2,1,0:T(8,128)(2,1)}) custom-call(f32[1,128]{1,0:T(1,128)S(1)} %get-tuple-element.12.refs_0_, bf16[128,256]{1,0:T(8,128)(2,1)S(1)} %get-tuple-element.13.refs_1_, bf16[128,256]{1,0:T(8,128)(2,1)S(1)} %get-tuple-element.14.refs_2_, ...), custom_call_target="tpu_custom_call" | custom-call | tf_op jit(solution)/shard_map/pallas_call | solution.py:694
